TPU v7x, 32 devices: a whole 2x2x4 slice. The times are simulated.
32 devices in a mesh: len: 16 (over z, x, core), dep: 2 (over y).
Axes of the slice: x: 2, y: 2, z: 4, core: 2. Of those that a mesh axis runs over, the one named last changes fastest.
Arguments:
- forward_states: bfloat16 [3, 19, 128, 16, 256], P(None, None, 'len', 'dep'), may hold values from 0 to 1, as said below
- adjoint_end: float32 [19, 128, 16, 256], P(None, 'len', 'dep'), may hold values from -6 to 6
- cell_kind: int32 [128, 16, 256], P('len', 'dep'), may hold values from 0 to 2
- basis_len: float32 [128, 64], P('len'), may hold values from -1 to 1
- basis_dep: float32 [16, 64], P('dep'), may hold values from -3 to 3
- basis_span: float32 [256, 32], replicated, may hold values from -0.75 to 0.75
Outputs:
- adjoint_start: float32 [19, 128, 16, 256], P(None, 'len', 'dep')
- coefficients: float32 [64, 64, 32], P('len', 'dep')
Inputs may be any that keep to these rules, and one draw needn't show every extreme that they name: `forward_states`: every population is positive and each cell's populations sum to between 0.5 and 1.6.
All inputs are finite; a program needn't handle non-finite values.
Results may differ from a plain program's by a relative error of at most 0.0003.
Values sent between devices are 32-bit elements; how exact they have to be, the bound alone decides.
A program may use at most 64 MiB of HBM per device.

v0:
```python
import jax
import jax.numpy as jnp
from jax import lax
from jax.sharding import PartitionSpec as P

STEPS = 3


velocities = [
    (0, 0, 0),
    (1, 0, 0),
    (-1, 0, 0),
    (0, 1, 0),
    (0, -1, 0),
    (0, 0, 1),
    (0, 0, -1),
    (1, 1, 0),
    (-1, -1, 0),
    (1, -1, 0),
    (-1, 1, 0),
    (1, 0, 1),
    (-1, 0, -1),
    (1, 0, -1),
    (-1, 0, 1),
    (0, 1, 1),
    (0, -1, -1),
    (0, 1, -1),
    (0, -1, 1),
]
opposite = [0, 2, 1, 4, 3, 6, 5, 8, 7, 10, 9, 12, 11, 14, 13, 16, 15, 18, 17]
omega = 1.25


def padded_2(block, sides, width):
    for axis, dim in sides:
        count = lax.axis_size(axis)
        forward = [(i, i + 1) for i in range(count - 1)]
        forward.append((count - 1, 0))
        backward = [(target, source) for source, target in forward]
        low = lax.ppermute(
            lax.slice_in_dim(block, block.shape[dim] - width, None, axis=dim), axis, forward
        )
        high = lax.ppermute(lax.slice_in_dim(block, 0, width, axis=dim), axis, backward)
        block = jnp.concatenate([low, block, high], axis=dim)
    return block


def lattice_weight(vel):
    total = abs(vel[0]) + abs(vel[1]) + abs(vel[2])
    return 1.0 / 3.0 if total == 0 else 1.0 / 18.0 if total == 1 else 1.0 / 36.0


def collide_back(post, forward, kind):
    fwd = forward.astype(jnp.float32)
    rho = jnp.sum(fwd, axis=0)
    moment = [
        sum((float(vel[d]) * fwd[i] for i, vel in enumerate(velocities) if vel[d] != 0))
        for d in range(3)
    ]
    speed = [moment[d] / rho for d in range(3)]
    usq = speed[0] * speed[0] + speed[1] * speed[1] + speed[2] * speed[2]
    acc_rho = jnp.zeros_like(rho)
    acc_mom = [jnp.zeros_like(rho) for d in range(3)]
    sens = jnp.zeros_like(rho)
    for i, vel in enumerate(velocities):
        weight = lattice_weight(vel)
        along = (
            sum((float(vel[d]) * speed[d] for d in range(3) if vel[d] != 0))
            if i > 0
            else jnp.zeros_like(rho)
        )
        feq = weight * rho * (1.0 + 3.0 * along + 4.5 * along * along - 1.5 * usq)
        sens = sens + post[i] * (feq - fwd[i])
        weighted = weight * post[i]
        acc_rho = acc_rho + weighted * (1.0 - 4.5 * along * along + 1.5 * usq)
        for d in range(3):
            acc_mom[d] = acc_mom[d] + weighted * (
                3.0 * vel[d] + 9.0 * along * vel[d] - 3.0 * speed[d]
            )
    solid = kind == 2
    result = []
    for j, vel in enumerate(velocities):
        grad = acc_rho
        for d in range(3):
            if vel[d] != 0:
                grad = grad + float(vel[d]) * acc_mom[d]
        fluid_value = (1.0 - omega) * post[j] + omega * grad
        result.append(jnp.where(solid, post[opposite[j]], fluid_value))
    return (jnp.stack(result), jnp.where(solid, 0.0, sens))


def extend_rim(adjoint):
    return padded_2(adjoint, (("len", 1), ("dep", 2)), 1)


def on_device(forward_states, adjoint_end, cell_kind, basis_len, basis_dep, basis_span):
    cells_x, cells_y, cells_z = cell_kind.shape
    adjoint = adjoint_end
    surface = (cell_kind == 1).astype(jnp.float32)
    sens_total = jnp.zeros(cell_kind.shape, jnp.float32)
    for step in range(STEPS - 1, -1, -1):
        padded = extend_rim(adjoint)
        pulled = []
        for i, vel in enumerate(velocities):
            moved = padded[
                i, 1 + vel[0] : 1 + vel[0] + cells_x, 1 + vel[1] : 1 + vel[1] + cells_y, :
            ]
            if vel[2] != 0:
                moved = jnp.roll(moved, -vel[2], axis=2)
            if vel[0] != 0:
                moved = moved + 2.0 * vel[0] * surface
            pulled.append(moved)
        post = jnp.stack(pulled)
        adjoint, sens = collide_back(post, forward_states[step], cell_kind)
        sens_total = sens_total + sens
    span_part = jnp.dot(
        sens_total.reshape(cells_x * cells_y, cells_z),
        basis_span,
        preferred_element_type=jnp.float32,
        precision=lax.Precision.HIGHEST,
    ).reshape(cells_x, cells_y, -1)
    depth_part = jnp.einsum("xyr,yq->xqr", span_part, basis_dep, precision=lax.Precision.HIGHEST)
    count_len = lax.axis_size("len")
    count_dep = lax.axis_size("dep")
    partial_modes = jnp.einsum(
        "xqr,xp->pqr", depth_part, basis_len, precision=lax.Precision.HIGHEST
    )
    modes_x, modes_y, modes_z = partial_modes.shape
    arranged = partial_modes.reshape(
        count_len, modes_x // count_len, count_dep, modes_y // count_dep, modes_z
    )
    arranged = arranged.transpose(0, 2, 1, 3, 4).reshape(
        count_len * count_dep * (modes_x // count_len), modes_y // count_dep, modes_z
    )
    coefficients = lax.psum_scatter(arranged, ("len", "dep"), scatter_dimension=0, tiled=True)
    return (adjoint, coefficients)


def solution(mesh):
    return jax.shard_map(
        on_device,
        mesh=mesh,
        in_specs=(
            P(None, None, "len", "dep", None),
            P(None, "len", "dep", None),
            P("len", "dep", None),
            P("len", None),
            P("dep", None),
            P(),
        ),
        out_specs=(P(None, "len", "dep", None), P("len", "dep", None)),
        check_vma=False,
    )
```

profile of v0, /device:TPU:0, one launch (start us, length us, event | category | flops | bytes accessed | tf_op | source)
XLA Modules:
  0.0 222.9 jit_solution(8247210859217276112)
XLA Ops:
  7.2 1.0 fusion.647
  8.2 5.5 %collective-permute-start = (f32[19,1,8,256]{3,2,1,0:T(8,128)S(1)}, f32[19,1,8,256]{3,2,1,0:T(8,128)S(1)}, u32[]{:S(2)}, u32[]{:S(2)}) collective-permute-start(f32[19,1,8,256]{3,2,1,0:T(8,128)S(1)} %get-tuple-element.157), channel_id=1, source_target_pairs={{2,0},{4,2},{6,4},{8,6},{10,8},{12,10},{14,12},{16,14},{18,16},{20... | collective-permute-start | bytes 466952 | tf_op jit(solution)/shard_map/ppermute | solution.py:43
  13.7 0.9 slice_bitcast_fusion.63
  14.8 2.0 slice_convert_fusion
  16.8 0.1 copy-done.1
  16.8 0.3 fusion.2
  17.2 3.9 %collective-permute-done.1 = f32[19,1,8,256]{3,2,1,0:T(8,128)S(1)} collective-permute-done((f32[19,1,8,256]{3,2,1,0:T(8,128)S(1)}, f32[19,1,8,256]{3,2,1,0:T(8,128)S(1)}, u32[]{:S(2)}, u32[]{:S(2)}) %collective-permute-start.1) | collective-permute-done | bytes 155680 | tf_op jit(solution)/shard_map/ppermute | solution.py:40
  21.1 0.3 constant_dynamic-update-slice_fusion.5
  21.6 0.2 fusion.644
  21.8 1.6 collective-permute-start.3
  23.4 0.5 collective-permute-start.2
  24.1 0.1 slice.961
  24.2 3.4 %collective-permute-done.3 = f32[19,10,1,256]{3,2,1,0:T(1,128)S(1)} collective-permute-done((f32[19,10,1,256]{3,2,1,0:T(1,128)S(1)}, f32[19,10,1,256]{3,2,1,0:T(1,128)S(1)}, u32[]{:S(2)}, u32[]{:S(2)}) %collective-permute-start.3) | collective-permute-done | bytes 194592 | tf_op jit(solution)/shard_map/ppermute | solution.py:40
  27.5 2.1 collective-permute-done.2
  29.8 0.1 slice.971
  29.9 0.1 slice.973
  30.0 0.7 constant_dynamic-update-slice_fusion.25
  30.7 0.3 constant_dynamic-update-slice_fusion.24
  31.0 0.3 constant_dynamic-update-slice_fusion.22
  31.3 0.3 constant_dynamic-update-slice_fusion.20
  32.1 4.4 %collective-permute-start.4 = (f32[19,1,8,256]{3,2,1,0:T(8,128)S(1)}, f32[19,1,8,256]{3,2,1,0:T(8,128)S(1)}, u32[]{:S(2)}, u32[]{:S(2)}) collective-permute-start(f32[19,1,8,256]{3,2,1,0:T(8,128)S(1)} %get-tuple-element.151), channel_id=1, source_target_pairs={{2,0},{4,2},{6,4},{8,6},{10,8},{12,10},{14,12},{16,14},{18,16},{20... | collective-permute-start | bytes 466952 | tf_op jit(solution)/shard_map/ppermute | solution.py:43
  36.6 2.9 %collective-permute-done.5 = f32[19,1,8,256]{3,2,1,0:T(8,128)S(1)} collective-permute-done((f32[19,1,8,256]{3,2,1,0:T(8,128)S(1)}, f32[19,1,8,256]{3,2,1,0:T(8,128)S(1)}, u32[]{:S(2)}, u32[]{:S(2)}) %collective-permute-start.5) | collective-permute-done | bytes 155680 | tf_op jit(solution)/shard_map/ppermute | solution.py:40
  39.5 0.2 pad_maximum_fusion.3
  39.7 1.6 collective-permute-start.7
  41.3 0.5 collective-permute-start.6
  42.2 0.1 slice.1005
  42.3 4.0 %collective-permute-done.7 = f32[19,10,1,256]{3,2,1,0:T(1,128)S(1)} collective-permute-done((f32[19,10,1,256]{3,2,1,0:T(1,128)S(1)}, f32[19,10,1,256]{3,2,1,0:T(1,128)S(1)}, u32[]{:S(2)}, u32[]{:S(2)}) %collective-permute-start.7) | collective-permute-done | bytes 194592 | tf_op jit(solution)/shard_map/ppermute | solution.py:40
  46.3 2.1 collective-permute-done.6
  48.6 0.1 slice.1011
  48.7 0.1 slice.1013
  48.8 0.1 slice.1003
  48.9 0.7 constant_dynamic-update-slice_fusion.44
  49.5 0.3 constant_dynamic-update-slice_fusion.43
  49.8 0.3 constant_dynamic-update-slice_fusion.41
  50.2 0.3 constant_dynamic-update-slice_fusion.39
  50.9 4.4 %collective-permute-start.8 = (f32[19,1,8,256]{3,2,1,0:T(8,128)S(1)}, f32[19,1,8,256]{3,2,1,0:T(8,128)S(1)}, u32[]{:S(2)}, u32[]{:S(2)}) collective-permute-start(f32[19,1,8,256]{3,2,1,0:T(8,128)S(1)} %get-tuple-element.148), channel_id=1, source_target_pairs={{2,0},{4,2},{6,4},{8,6},{10,8},{12,10},{14,12},{16,14},{18,16},{20... | collective-permute-start | bytes 466952 | tf_op jit(solution)/shard_map/ppermute | solution.py:43
  55.4 2.9 %collective-permute-done.9 = f32[19,1,8,256]{3,2,1,0:T(8,128)S(1)} collective-permute-done((f32[19,1,8,256]{3,2,1,0:T(8,128)S(1)}, f32[19,1,8,256]{3,2,1,0:T(8,128)S(1)}, u32[]{:S(2)}, u32[]{:S(2)}) %collective-permute-start.9) | collective-permute-done | bytes 155680 | tf_op jit(solution)/shard_map/ppermute | solution.py:40
  58.3 0.2 pad_maximum_fusion
  58.5 1.6 collective-permute-start.11
  60.1 0.5 collective-permute-start.10
  61.0 0.1 slice.1045
  61.1 3.9 %collective-permute-done.11 = f32[19,10,1,256]{3,2,1,0:T(1,128)S(1)} collective-permute-done((f32[19,10,1,256]{3,2,1,0:T(1,128)S(1)}, f32[19,10,1,256]{3,2,1,0:T(1,128)S(1)}, u32[]{:S(2)}, u32[]{:S(2)}) %collective-permute-start.11) | collective-permute-done | bytes 194592 | tf_op jit(solution)/shard_map/ppermute | solution.py:40
  65.0 2.1 collective-permute-done.10
  67.4 0.1 slice.1053
  67.4 0.1 slice.1043
  67.5 0.6 constant_dynamic-update-slice_fusion.63
  68.2 1.9 fusion.75
  70.1 0.3 constant_dynamic-update-slice_fusion.62
  70.4 0.3 constant_dynamic-update-slice_fusion.60
  70.8 0.3 constant_dynamic-update-slice_fusion.58
  71.3 0.4 copy-done.15
  71.8 0.4 convolution_bitcast_fusion.1
  72.2 0.6 copy-done.16
  72.8 1.8 convolution_bitcast_fusion
  74.6 0.9 copy.11
  75.6 1.2 reshape.131
  76.8 2.4 %copy.12 = f32[16,2,4,32,32]{4,3,2,1,0:T(8,128)} copy(f32[16,2,4,32,32]{3,1,4,2,0:T(2,128)S(1)} %bitcast.1062) | data formatting | bytes 1048576 | tf_op jit(solution)/shard_map/transpose | solution.py:132
  79.2 0.8 copy-done.8
  80.0 0.6 constant_dynamic-update-slice_fusion.49
  80.7 0.7 constant_dynamic-update-slice_fusion.48
  81.3 0.7 constant_dynamic-update-slice_fusion.47
  82.0 0.7 constant_dynamic-update-slice_fusion.46
  82.6 0.7 constant_dynamic-update-slice_fusion.45
  83.3 132.8 %reduce-scatter.2.cloned.1.call-done = f32[4,32,32]{2,1,0:T(8,128)} async-done(((f32[128,32,32]{2,1,0:T(8,128)}), f32[4,32,32]{2,1,0:T(8,128)}) %reduce-scatter.2.cloned.1.call-update) | async-done | bytes 16400 | tf_op jit(solution)/shard_map/reduce_scatter | solution.py:135
  (124 shorter events, 3.3 us)
Async XLA Ops:
  7.2 61.1 %copy-start = (f32[256,32]{0,1:T(8,128)S(1)}, f32[256,32]{0,1:T(8,128)}, u32[]{:S(2)}) copy-start(f32[256,32]{0,1:T(8,128)} %param.11) | copy-start | bytes 98308
  7.2 208.9 %reduce-scatter.2.cloned.1.call-start = ((), (), s32[]{:S(2)}) async-start(), calls=%async_computation.1 | async-start | bytes 2162688 | tf_op jit(solution)/shard_map/reduce_scatter | solution.py:135
  8.2 13.2 %collective-permute-start = (f32[19,1,8,256]{3,2,1,0:T(8,128)S(1)}, f32[19,1,8,256]{3,2,1,0:T(8,128)S(1)}, u32[]{:S(2)}, u32[]{:S(2)}) collective-permute-start(f32[19,1,8,256]{3,2,1,0:T(8,128)S(1)} %get-tuple-element.157), channel_id=1, source_target_pairs={{2,0},{4,2},{6,4},{8,6},{10,8},{12,10},{14,12},{16,14},{18,16},{20... | collective-permute-start | bytes 466952 | tf_op jit(solution)/shard_map/ppermute | solution.py:43
  13.7 7.4 %collective-permute-start.1 = (f32[19,1,8,256]{3,2,1,0:T(8,128)S(1)}, f32[19,1,8,256]{3,2,1,0:T(8,128)S(1)}, u32[]{:S(2)}, u32[]{:S(2)}) collective-permute-start(f32[19,1,8,256]{3,2,1,0:T(8,128)S(1)} %get-tuple-element.158), channel_id=1, source_target_pairs={{0,2},{2,4},{4,6},{6,8},{8,10},{10,12},{12,14},{14,16},{16,18},{18... | collective-permute-start | bytes 466952 | tf_op jit(solution)/shard_map/ppermute | solution.py:40
  14.8 2.1 copy-start.1
  16.8 4.2 %copy-start.2 = (f32[19,8,8,256]{3,2,1,0:T(8,128)S(1)}, f32[19,8,8,256]{3,2,1,0:T(8,128)}, u32[]{:S(2)}) copy-start(f32[19,8,8,256]{3,2,1,0:T(8,128)} %param.7) | copy-start | bytes 3735556
  21.8 5.7 %collective-permute-start.3 = (f32[19,10,1,256]{3,2,1,0:T(1,128)S(1)}, f32[19,10,1,256]{3,2,1,0:T(1,128)S(1)}, u32[]{:S(2)}, u32[]{:S(2)}) collective-permute-start(f32[19,10,1,256]{3,2,1,0:T(1,128)S(1)} %get-tuple-element.134), channel_id=1, source_target_pairs={{0,1},{1,0},{2,3},{3,2},{4,5},{5,4},{6,7},{7,6},{8,9},{9,8},{10,11... | collective-permute-start | bytes 583688 | tf_op jit(solution)/shard_map/ppermute | solution.py:40
  23.4 6.2 %collective-permute-start.2 = (f32[19,10,1,256]{3,2,1,0:T(1,128)S(1)}, f32[19,10,1,256]{3,2,1,0:T(1,128)S(1)}, u32[]{:S(2)}, u32[]{:S(2)}) collective-permute-start(f32[19,10,1,256]{3,2,1,0:T(1,128)S(1)} %get-tuple-element.135), channel_id=1, source_target_pairs={{1,0},{0,1},{3,2},{2,3},{5,4},{4,5},{7,6},{6,7},{9,8},{8,9},{11,10... | collective-permute-start | bytes 583688 | tf_op jit(solution)/shard_map/ppermute | solution.py:43
  24.2 5.8 %copy-start.13 = (s32[8,8,256]{2,1,0:T(8,128)S(1)}, s32[8,8,256]{2,1,0:T(8,128)}, u32[]{:S(2)}) copy-start(s32[8,8,256]{2,1,0:T(8,128)} %param.8) | copy-start | bytes 196612
  32.1 7.4 %collective-permute-start.5 = (f32[19,1,8,256]{3,2,1,0:T(8,128)S(1)}, f32[19,1,8,256]{3,2,1,0:T(8,128)S(1)}, u32[]{:S(2)}, u32[]{:S(2)}) collective-permute-start(f32[19,1,8,256]{3,2,1,0:T(8,128)S(1)} %get-tuple-element.150), channel_id=1, source_target_pairs={{0,2},{2,4},{4,6},{6,8},{8,10},{10,12},{12,14},{14,16},{16,18},{18... | collective-permute-start | bytes 466952 | tf_op jit(solution)/shard_map/ppermute | solution.py:40
  32.1 7.3 %collective-permute-start.4 = (f32[19,1,8,256]{3,2,1,0:T(8,128)S(1)}, f32[19,1,8,256]{3,2,1,0:T(8,128)S(1)}, u32[]{:S(2)}, u32[]{:S(2)}) collective-permute-start(f32[19,1,8,256]{3,2,1,0:T(8,128)S(1)} %get-tuple-element.151), channel_id=1, source_target_pairs={{2,0},{4,2},{6,4},{8,6},{10,8},{12,10},{14,12},{16,14},{18,16},{20... | collective-permute-start | bytes 466952 | tf_op jit(solution)/shard_map/ppermute | solution.py:43
  39.7 6.6 %collective-permute-start.7 = (f32[19,10,1,256]{3,2,1,0:T(1,128)S(1)}, f32[19,10,1,256]{3,2,1,0:T(1,128)S(1)}, u32[]{:S(2)}, u32[]{:S(2)}) collective-permute-start(f32[19,10,1,256]{3,2,1,0:T(1,128)S(1)} %get-tuple-element.130), channel_id=1, source_target_pairs={{0,1},{1,0},{2,3},{3,2},{4,5},{5,4},{6,7},{7,6},{8,9},{9,8},{10,11... | collective-permute-start | bytes 583688 | tf_op jit(solution)/shard_map/ppermute | solution.py:40
  41.3 7.1 %collective-permute-start.6 = (f32[19,10,1,256]{3,2,1,0:T(1,128)S(1)}, f32[19,10,1,256]{3,2,1,0:T(1,128)S(1)}, u32[]{:S(2)}, u32[]{:S(2)}) collective-permute-start(f32[19,10,1,256]{3,2,1,0:T(1,128)S(1)} %get-tuple-element.131), channel_id=1, source_target_pairs={{1,0},{0,1},{3,2},{2,3},{5,4},{4,5},{7,6},{6,7},{9,8},{8,9},{11,10... | collective-permute-start | bytes 583688 | tf_op jit(solution)/shard_map/ppermute | solution.py:43
  50.9 7.4 %collective-permute-start.9 = (f32[19,1,8,256]{3,2,1,0:T(8,128)S(1)}, f32[19,1,8,256]{3,2,1,0:T(8,128)S(1)}, u32[]{:S(2)}, u32[]{:S(2)}) collective-permute-start(f32[19,1,8,256]{3,2,1,0:T(8,128)S(1)} %get-tuple-element.147), channel_id=1, source_target_pairs={{0,2},{2,4},{4,6},{6,8},{8,10},{10,12},{12,14},{14,16},{16,18},{18... | collective-permute-start | bytes 466952 | tf_op jit(solution)/shard_map/ppermute | solution.py:40
  50.9 7.3 %collective-permute-start.8 = (f32[19,1,8,256]{3,2,1,0:T(8,128)S(1)}, f32[19,1,8,256]{3,2,1,0:T(8,128)S(1)}, u32[]{:S(2)}, u32[]{:S(2)}) collective-permute-start(f32[19,1,8,256]{3,2,1,0:T(8,128)S(1)} %get-tuple-element.148), channel_id=1, source_target_pairs={{2,0},{4,2},{6,4},{8,6},{10,8},{12,10},{14,12},{16,14},{18,16},{20... | collective-permute-start | bytes 466952 | tf_op jit(solution)/shard_map/ppermute | solution.py:43
  58.5 6.4 %collective-permute-start.11 = (f32[19,10,1,256]{3,2,1,0:T(1,128)S(1)}, f32[19,10,1,256]{3,2,1,0:T(1,128)S(1)}, u32[]{:S(2)}, u32[]{:S(2)}) collective-permute-start(f32[19,10,1,256]{3,2,1,0:T(1,128)S(1)} %get-tuple-element.126), channel_id=1, source_target_pairs={{0,1},{1,0},{2,3},{3,2},{4,5},{5,4},{6,7},{7,6},{8,9},{9,8},{10,11... | collective-permute-start | bytes 583688 | tf_op jit(solution)/shard_map/ppermute | solution.py:40
  60.1 6.9 %collective-permute-start.10 = (f32[19,10,1,256]{3,2,1,0:T(1,128)S(1)}, f32[19,10,1,256]{3,2,1,0:T(1,128)S(1)}, u32[]{:S(2)}, u32[]{:S(2)}) collective-permute-start(f32[19,10,1,256]{3,2,1,0:T(1,128)S(1)} %get-tuple-element.127), channel_id=1, source_target_pairs={{1,0},{0,1},{3,2},{2,3},{5,4},{4,5},{7,6},{6,7},{9,8},{8,9},{11,10... | collective-permute-start | bytes 583688 | tf_op jit(solution)/shard_map/ppermute | solution.py:43
  68.2 2.6 %copy-start.3 = (f32[8,8,256]{2,1,0:T(8,128)}, f32[8,8,256]{2,1,0:T(8,128)S(1)}, u32[]{:S(2)}) copy-start(f32[8,8,256]{2,1,0:T(8,128)S(1)} %get-tuple-element.30) | copy-start | bytes 196612
  68.2 2.6 %copy-start.5 = (f32[8,8,256]{2,1,0:T(8,128)}, f32[8,8,256]{2,1,0:T(8,128)S(1)}, u32[]{:S(2)}) copy-start(f32[8,8,256]{2,1,0:T(8,128)S(1)} %get-tuple-element.31) | copy-start | bytes 196612
  68.2 3.1 %copy-start.7 = (f32[8,8,256]{2,1,0:T(8,128)}, f32[8,8,256]{2,1,0:T(8,128)S(1)}, u32[]{:S(2)}) copy-start(f32[8,8,256]{2,1,0:T(8,128)S(1)} %get-tuple-element.28) | copy-start | bytes 196612
  68.2 3.1 %copy-start.9 = (f32[8,8,256]{2,1,0:T(8,128)}, f32[8,8,256]{2,1,0:T(8,128)S(1)}, u32[]{:S(2)}) copy-start(f32[8,8,256]{2,1,0:T(8,128)S(1)} %get-tuple-element.29) | copy-start | bytes 196612
  70.4 0.8 copy-start.11
  71.1 0.7 copy-start.15
  71.1 1.7 copy-start.14
  71.8 1.0 copy-start.16
  79.1 0.8 copy-start.8
  79.1 0.9 copy-start.10
  79.1 0.9 copy-start.12
  79.1 1.5 copy-start.4
  79.1 1.5 copy-start.6
Sparse Core Ops, SparseCore 0:
  79.3 136.7 reduce-scatter.1
where the time goes:
time: 223 us
  waiting for transfers between devices  160 us (72%)
  starting transfers between devices  20.8 us (9%)
  between operations  14.7 us (7%)
  other arithmetic  11.9 us (5%)
  local copies, waits for them, and re-layouts  11.4 us (5%)
  matrix products  4.1 us (2%)
    reduce_scatter x1, waiting for transfers between devices, on_device(): lax.psum_scatter(arranged, ('len', 'dep'), scatter_dimension=0, tiled=True)  133 us
    ppermute x6, waiting for transfers between devices, padded_2(): lax.ppermute(lax.slice_in_dim(block, block.shape[dim] - width, None, axis...  21 us
    ppermute x6, starting transfers between devices, padded_2(): lax.ppermute(lax.slice_in_dim(block, 0, width, axis=dim), axis, backward)  15.8 us
    unnamed x54, other arithmetic  8.21 us
    ppermute x6, waiting for transfers between devices, padded_2(): lax.ppermute(lax.slice_in_dim(block, 0, width, axis=dim), axis, backward)  6.26 us
    ppermute x6, starting transfers between devices, padded_2(): lax.ppermute(lax.slice_in_dim(block, block.shape[dim] - width, None, axis...  4.87 us
  transfers between devices with their start and end apart: 13, of which 10 were waited for; matrix products, arithmetic and copies ran while one was open for 4% of the time, Pallas kernels for 0%

commit v1 on v0

v1 whole, which is shorter than its diff:
```python
import functools

import jax
import jax.numpy as jnp
from jax import lax
from jax.experimental import pallas as pl
from jax.experimental.pallas import tpu as pltpu
from jax.sharding import PartitionSpec as P

STEPS = 3
MESH = pl.DeviceIdType.MESH

velocities = [
    (0, 0, 0),
    (1, 0, 0),
    (-1, 0, 0),
    (0, 1, 0),
    (0, -1, 0),
    (0, 0, 1),
    (0, 0, -1),
    (1, 1, 0),
    (-1, -1, 0),
    (1, -1, 0),
    (-1, 1, 0),
    (1, 0, 1),
    (-1, 0, -1),
    (1, 0, -1),
    (-1, 0, 1),
    (0, 1, 1),
    (0, -1, -1),
    (0, 1, -1),
    (0, -1, 1),
]
omega = 1.25
COUNT = len(velocities)
PAIRS = [(i, i + 1) for i in range(1, COUNT, 2)]
ORDER = (
    [i for i, v in enumerate(velocities) if v[0] == 1]
    + [i for i, v in enumerate(velocities) if v[0] == -1]
    + [i for i, v in enumerate(velocities) if v[0] == 0]
)
PLACE = {i: k for k, i in enumerate(ORDER)}
SIGNS = (1, -1)
Y_POPS = [[i for i, v in enumerate(velocities) if v[1] == sign] for sign in SIGNS]
CORNERS = [i for i, v in enumerate(velocities) if v[0] != 0 and v[1] != 0]


def exact_dot(a, b, dims=((1,), (0,))):
    return lax.dot_general(
        a,
        b,
        (dims, ((), ())),
        precision=lax.Precision.HIGHEST,
        preferred_element_type=jnp.float32,
    )


def one_hot(shape, test):
    rows = lax.broadcasted_iota(jnp.int32, shape, 0)
    cols = lax.broadcasted_iota(jnp.int32, shape, 1)
    return jnp.where(test(rows, cols), 1.0, 0.0)


def kernel(
    sizes,
    fwd_hbm,
    adj_hbm,
    kind_ref,
    len_ref,
    dep_ref,
    span_ref,
    out_ref,
    coef_ref,
    adj,
    fwd,
    gap,
    speeds,
    ysend,
    yhalo,
    csend,
    chalo,
    sens,
    tbuf,
    tgot,
    rgot,
    depgot,
    span_wide,
    len_wide,
    load_sem,
    fwd_sem,
    x_sems,
    y_sems,
    c_sems,
    t_sems,
    r_sems,
    b_sems,
):
    count_len, count_dep, nx, ny, nz, mx, my, mz = sizes
    at_len = lax.axis_index("len")
    at_dep = lax.axis_index("dep")
    own_p, own_q = mx // count_len, my // count_dep
    fold = 128 // mz
    highs = ny // fold
    piece = tbuf.shape[1]

    def device(shift_len, shift_dep):
        return (
            lax.rem(at_len + (shift_len % count_len), count_len),
            lax.rem(at_dep + (shift_dep % count_dep), count_dep),
        )

    loads = [
        pltpu.make_async_copy(adj_hbm.at[i], adj.at[0, k, pl.ds(1, nx)], load_sem)
        for k, i in enumerate(ORDER)
    ]
    for copy in loads:
        copy.start()
    fwd_loads = [
        pltpu.make_async_copy(fwd_hbm.at[t], fwd.at[t], fwd_sem.at[t]) for t in range(STEPS)
    ]
    for t in range(STEPS - 1, -1, -1):
        fwd_loads[t].start()

    peers = {(k, 0) for k in range(1, count_len)} | {(0, k) for k in range(1, count_dep)}
    peers |= {(a % count_len, b % count_dep) for a in SIGNS for b in SIGNS}
    barrier = pltpu.get_barrier_semaphore()
    for peer in sorted(peers):
        pl.semaphore_signal(barrier, inc=1, device_id=device(*peer), device_id_type=MESH)

    def remote(src, dst, sems, index, target):
        return pltpu.make_async_remote_copy(
            src_ref=src,
            dst_ref=dst,
            send_sem=sems.at[(0,) + index],
            recv_sem=sems.at[(1,) + index],
            device_id=target,
            device_id_type=MESH,
        )

    def halo_copies(step):
        x_copies, y_copies, c_copies = [], [], []
        for side, sign in enumerate(SIGNS):
            pops = pl.ds(5 * side, 5)
            x_copies.append(
                remote(
                    adj.at[step, pops, 1 if sign == 1 else nx],
                    adj.at[step, pops, nx + 1 if sign == 1 else 0],
                    x_sems,
                    (step, side),
                    device(-sign, 0),
                )
            )
            y_copies.append(
                remote(
                    ysend.at[step, side],
                    yhalo.at[step, side],
                    y_sems,
                    (step, side),
                    device(0, -sign),
                )
            )
        for k, i in enumerate(CORNERS):
            vel = velocities[i]
            c_copies.append(
                remote(
                    csend.at[step, k],
                    chalo.at[step, k],
                    c_sems,
                    (step, k),
                    device(-vel[0], -vel[1]),
                )
            )
        return x_copies, y_copies, c_copies

    def fill_corners(step):
        for k, i in enumerate(CORNERS):
            vel = velocities[i]
            side = SIGNS.index(vel[1])
            row = 0 if vel[0] == 1 else nx - 1
            csend[step, k] = ysend[step, side, Y_POPS[side].index(i), pl.ds(row, 1), :]

    def fill_rows(step, i, x, value):
        vel = velocities[i]
        if vel[1] != 0:
            side = SIGNS.index(vel[1])
            row = value[0:1, :] if vel[1] == 1 else value[ny - 1 : ny, :]
            ysend[step, side, Y_POPS[side].index(i), pl.ds(x, 1), :] = row

    copies = [halo_copies(step) for step in range(STEPS)]

    def send(step):
        for group in copies[step]:
            for copy in group:
                copy.start()

    pltpu.make_async_copy(adj_hbm, adj.at[0, :, pl.ds(1, nx)], load_sem).wait()

    def first_rows(x, carry):
        for pops in Y_POPS:
            for i in pops:
                fill_rows(0, i, x, adj[0, PLACE[i], x + 1])
        return carry

    lax.fori_loop(0, nx, first_rows, 0)
    fill_corners(0)
    pl.semaphore_wait(barrier, len(peers))
    send(0)
    basis_copies = [
        remote(dep_ref, depgot.at[k], b_sems, (k,), device(0, k)) for k in range(1, count_dep)
    ]
    for copy in basis_copies:
        copy.start()

    def prepare(t):
        def plane(x, carry):
            f = [fwd[t, i, x].astype(jnp.float32) for i in range(COUNT)]
            sums = [f[i] + f[o] for i, o in PAIRS]
            difs = [f[i] - f[o] for i, o in PAIRS]
            rho = f[0]
            for part in sums:
                rho = rho + part
            inverse = 1.0 / rho
            speed = []
            for d in range(3):
                moment = None
                for (i, o), dif in zip(PAIRS, difs):
                    c = velocities[i][d]
                    if c != 0:
                        if moment is None:
                            moment = dif
                        else:
                            moment = moment + dif if c > 0 else moment - dif
                speed.append(moment * inverse)
                speeds[t, d, x] = speed[d]
            usq = speed[0] * speed[0] + speed[1] * speed[1] + speed[2] * speed[2]
            base = rho * (1.0 - 1.5 * usq)
            gap[t, 0, x] = (1.0 / 3.0) * base - f[0]
            for i, o in PAIRS:
                vel = velocities[i]
                terms = [(speed[d], vel[d]) for d in range(3) if vel[d] != 0]
                along = terms[0][0]
                if len(terms) == 2:
                    along = along + terms[1][0] if terms[1][1] > 0 else along - terms[1][0]
                weight = 1.0 / 18.0 if len(terms) == 1 else 1.0 / 36.0
                mass = weight * rho * along
                even = weight * base + 4.5 * mass * along
                odd = 3.0 * mass
                gap[t, i, x] = even + odd - f[i]
                gap[t, o, x] = even - odd - f[o]
            return carry

        fwd_loads[t].wait()
        lax.fori_loop(0, nx, plane, 0)

    rows_of = lax.broadcasted_iota(jnp.int32, (ny, nz), 0)

    def collide(step, x, edge):
        t = STEPS - 1 - step
        kind = kind_ref[x]
        solid = kind == 2
        push = jnp.where(kind == 1, 2.0, 0.0)
        post = []
        for i, vel in enumerate(velocities):
            value = adj[step, PLACE[i], x + (1 + vel[0])]
            if vel[1] != 0:
                side = SIGNS.index(vel[1])
                j = Y_POPS[side].index(i)
                if vel[0] != 0 and edge:
                    at = x + vel[0]
                    inside = (at >= 0) & (at < nx)
                    near = yhalo[step, side, j, pl.ds(jnp.clip(at, 0, nx - 1), 1), :]
                    row = jnp.where(inside, near, chalo[step, CORNERS.index(i)])
                else:
                    row = yhalo[step, side, j, pl.ds(x + vel[0], 1), :]
                if vel[1] == 1:
                    value = jnp.where(rows_of == ny - 1, row, pltpu.roll(value, ny - 1, 0))
                else:
                    value = jnp.where(rows_of == 0, row, pltpu.roll(value, 1, 0))
            if vel[2] != 0:
                value = pltpu.roll(value, (-vel[2]) % nz, 1)
            if vel[0] == 1:
                value = value + push
            elif vel[0] == -1:
                value = value - push
            post.append(value)

        change = post[0] * gap[t, 0, x]
        for i in range(1, COUNT):
            change = change + post[i] * gap[t, i, x]
        where = pl.ds(pl.multiple_of(x * ny, ny), ny)
        if step == 0:
            sens[where, :] = change
        elif step < STEPS - 1:
            sens[where, :] = sens[where, :] + change
        else:
            sens[where, :] = jnp.where(solid, 0.0, sens[where, :] + change)

        s = {i: post[i] + post[o] for i, o in PAIRS}
        d = {i: post[i] - post[o] for i, o in PAIRS}
        ux, uy, uz = (speeds[t, k, x] for k in range(3))
        xy, xz, yz = s[7] + s[9], s[11] + s[13], s[15] + s[17]
        sx, sy, sz = 2.0 * s[1], 2.0 * s[3], 2.0 * s[5]
        m0 = 12.0 * post[0] + (sx + sy + sz) + (xy + xz + yz)
        mxx, myy, mzz = sx + xy + xz, sy + xy + yz, sz + xz + yz
        mxy, mxz, myz = s[7] - s[9], s[11] - s[13], s[15] - s[17]
        m1x = 2.0 * d[1] + (d[7] + d[9]) + (d[11] + d[13])
        m1y = 2.0 * d[3] + (d[7] - d[9]) + (d[15] + d[17])
        m1z = 2.0 * d[5] + (d[11] - d[13]) + (d[15] - d[17])
        bx = mxx * ux + mxy * uy + mxz * uz
        by = mxy * ux + myy * uy + myz * uz
        bz = mxz * ux + myz * uy + mzz * uz
        usq = ux * ux + uy * uy + uz * uz
        along = ux * bx + uy * by + uz * bz
        acc_rho = (omega / 36.0) * (m0 * (1.0 + 1.5 * usq) - 4.5 * along)
        acc = [
            (omega / 12.0) * (m + 3.0 * b - u * m0)
            for m, b, u in ((m1x, bx, ux), (m1y, by, uy), (m1z, bz, uz))
        ]

        def store(i, value):
            if step == STEPS - 1:
                out_ref[i, x] = value
            else:
                adj[step + 1, PLACE[i], x + 1] = value
                fill_rows(step + 1, i, x, value)

        store(0, jnp.where(solid, post[0], (1.0 - omega) * post[0] + acc_rho))
        for i, o in PAIRS:
            vel = velocities[i]
            terms = [(acc[k], vel[k]) for k in range(3) if vel[k] != 0]
            grad = terms[0][0]
            if len(terms) == 2:
                grad = grad + terms[1][0] if terms[1][1] > 0 else grad - terms[1][0]
            store(i, jnp.where(solid, post[o], (1.0 - omega) * post[i] + (acc_rho + grad)))
            store(o, jnp.where(solid, post[i], (1.0 - omega) * post[o] + (acc_rho - grad)))

    prepare(STEPS - 1)
    spread = one_hot((mz, 128), lambda r, c: lax.rem(c, mz) == r)
    span_wide[...] = exact_dot(span_ref[...], spread)
    total = count_len * piece
    pick = one_hot(
        (total, mx),
        lambda r, c: (lax.div(r, piece) * own_p + lax.div(lax.rem(r, piece), highs) == c)
        & (lax.rem(r, piece) < own_p * highs),
    )
    lens = exact_dot(pick, len_ref[...], ((1,), (1,)))
    cells = one_hot((nx, nx * ny), lambda r, c: lax.div(c, ny) == r)
    halves = one_hot(
        (total, nx * ny),
        lambda r, c: lax.div(lax.rem(c, ny), fold) == lax.rem(lax.rem(r, piece), highs),
    )
    len_wide[...] = exact_dot(lens, cells) * halves

    for step in range(STEPS):
        x_copies, y_copies, c_copies = copies[step]
        for copy in y_copies:
            copy.wait_recv()

        def inner(x, carry):
            collide(step, x, False)
            return carry

        lax.fori_loop(1, nx - 1, inner, 0)
        for copy in x_copies + c_copies:
            copy.wait_recv()

        def outer(k, carry):
            collide(step, k * (nx - 1), True)
            return carry

        lax.fori_loop(0, 2, outer, 0)
        if step < STEPS - 1:
            fill_corners(step + 1)
            send(step + 1)
            prepare(STEPS - 2 - step)

    narrow = exact_dot(sens[...], span_wide[...])
    keep = one_hot(
        (nx * ny, 128), lambda r, c: lax.rem(lax.rem(r, ny), fold) == lax.div(c, mz)
    )
    partial = exact_dot(len_wide[...], narrow * keep)
    tbuf[...] = partial.reshape(tbuf.shape)
    t_copies = [
        remote(tbuf.at[device(k, 0)[0]], tgot.at[k], t_sems, (k,), device(k, 0))
        for k in range(1, count_len)
    ]
    for copy in t_copies:
        copy.start()

    for copy in basis_copies:
        copy.wait_recv()
    width = fold * piece
    mine = one_hot(
        (own_p * own_q, my), lambda r, c: lax.rem(r, own_q) + at_dep * own_q == c
    )
    lay = one_hot(
        (ny, width),
        lambda r, c: lax.rem(lax.rem(c, piece), highs) * fold + lax.div(c, piece) == r,
    )
    match = one_hot(
        (own_p * own_q, width),
        lambda r, c: lax.div(lax.rem(c, piece), highs) == lax.div(r, own_q),
    )
    deps = [
        exact_dot(
            exact_dot(mine, dep_ref[...] if k == 0 else depgot[k], ((1,), (1,))), lay
        )
        * match
        for k in range(count_dep)
    ]

    reduced = tbuf[at_len]
    for k in range(1, count_len):
        t_copies[k - 1].wait_recv()
        reduced = reduced + tgot[k]
    rgot[0] = reduced
    r_copies = [
        remote(rgot.at[0], rgot.at[k], r_sems, (k,), device(0, k)) for k in range(1, count_dep)
    ]
    for copy in r_copies:
        copy.start()

    def depth_modes(k):
        held = rgot[k]
        tall = jnp.concatenate(
            [held if j == 0 else pltpu.roll(held, 128 - j * mz, 1) for j in range(fold)], axis=0
        )
        return exact_dot(deps[k], tall)

    modes = depth_modes(0)
    for k in range(1, count_dep):
        r_copies[k - 1].wait_recv()
        modes = modes + depth_modes(k)
    coef_ref[...] = modes[:, :mz].reshape(coef_ref.shape)

    for step in range(STEPS):
        for group in copies[step]:
            for copy in group:
                copy.wait_send()
    for copy in basis_copies + t_copies + r_copies:
        copy.wait_send()


def on_device(forward_states, adjoint_end, cell_kind, basis_len, basis_dep, basis_span):
    count_len = lax.axis_size("len")
    count_dep = lax.axis_size("dep")
    nx, ny, nz = cell_kind.shape
    mx, my, mz = basis_len.shape[1], basis_dep.shape[1], basis_span.shape[1]
    sizes = (count_len, count_dep, nx, ny, nz, mx, my, mz)
    own_p = mx // count_len
    highs = ny // (128 // mz)
    piece = -(-own_p * highs // 8) * 8
    f32 = jnp.float32
    dma = pltpu.SemaphoreType.DMA
    vmem = pl.BlockSpec(memory_space=pltpu.VMEM)
    hbm = pl.BlockSpec(memory_space=pl.ANY)
    return pl.pallas_call(
        functools.partial(kernel, sizes),
        out_shape=(
            jax.ShapeDtypeStruct((COUNT, nx, ny, nz), f32),
            jax.ShapeDtypeStruct((own_p, my // count_dep, mz), f32),
        ),
        in_specs=[hbm, hbm, vmem, vmem, vmem, vmem],
        out_specs=(vmem, vmem),
        scratch_shapes=[
            pltpu.VMEM((STEPS, COUNT, nx + 2, ny, nz), f32),
            pltpu.VMEM(forward_states.shape, forward_states.dtype),
            pltpu.VMEM((STEPS, COUNT, nx, ny, nz), f32),
            pltpu.VMEM((STEPS, 3, nx, ny, nz), f32),
            pltpu.VMEM((STEPS, 2, 5, nx, nz), f32),
            pltpu.VMEM((STEPS, 2, 5, nx, nz), f32),
            pltpu.VMEM((STEPS, 4, 1, nz), f32),
            pltpu.VMEM((STEPS, 4, 1, nz), f32),
            pltpu.VMEM((nx * ny, nz), f32),
            pltpu.VMEM((count_len, piece, 128), f32),
            pltpu.VMEM((count_len, piece, 128), f32),
            pltpu.VMEM((count_dep, piece, 128), f32),
            pltpu.VMEM((count_dep, ny, my), f32),
            pltpu.VMEM((nz, 128), f32),
            pltpu.VMEM((count_len * piece, nx * ny), f32),
            dma,
            dma((STEPS,)),
            dma((2, STEPS, 2)),
            dma((2, STEPS, 2)),
            dma((2, STEPS, 4)),
            dma((2, count_len)),
            dma((2, count_dep)),
            dma((2, count_dep)),
        ],
        compiler_params=pltpu.CompilerParams(
            collective_id=0, has_side_effects=True, vmem_limit_bytes=48 * 1024 * 1024
        ),
        cost_estimate=pl.CostEstimate(
            flops=STEPS * 600 * nx * ny * nz, bytes_accessed=5 * 1024 * 1024, transcendentals=0
        ),
    )(forward_states, adjoint_end, cell_kind, basis_len, basis_dep, basis_span)


def solution(mesh):
    return jax.shard_map(
        on_device,
        mesh=mesh,
        in_specs=(
            P(None, None, "len", "dep", None),
            P(None, "len", "dep", None),
            P("len", "dep", None),
            P("len", None),
            P("dep", None),
            P(),
        ),
        out_specs=(P(None, "len", "dep", None), P("len", "dep", None)),
        check_vma=False,
    )
```

time: 223 us -> 39.3 us (0.18)
  waiting for transfers between devices: 160 us -> 0 us
  Pallas kernels: 0 us -> 30.7 us
  starting transfers between devices: 20.8 us -> 0 us
  between operations: 14.7 us -> 0.65 us
  other arithmetic: 11.9 us -> 0 us
  matrix products: 4.1 us -> 0 us
  local copies, waits for them, and re-layouts: 11.4 us -> 7.53 us
    reduce_scatter x1 -> x0, waiting for transfers between devices: 133 us -> none  [on_device(): lax.psum_scatter(arranged, ('len', 'dep'), scatter_dimension=0, tiled=True)]
    pallas_call x0 -> x1, Pallas kernels: none -> 30.7 us  [on_device(): pl.pallas_call(functools.partial(kernel, sizes), out_shape=(jax.ShapeDtyp...]
    ppermute x12 -> x0, waiting for transfers between devices: 27.3 us -> none  [the longest x6 21 us: padded_2(): lax.ppermute(lax.slice_in_dim(block, block.shape[dim] - width, None, axis...]
    ppermute x12 -> x0, starting transfers between devices: 20.7 us -> none  [the longest x6 15.8 us: padded_2(): lax.ppermute(lax.slice_in_dim(block, 0, width, axis=dim), axis, backward)]
    unnamed x54 -> x0, other arithmetic: 8.21 us -> none
    unnamed x36 -> x13, local copies, waits for them, and re-layouts: 2.37 us -> 7.53 us
    dot_general x3 -> x0, matrix products: 4.1 us -> none  [the longest x1 1.86 us: on_device(): jnp.dot(sens_total.reshape(cells_x * cells_y, cells_z), basis_span, prefe...]
    slice x49 -> x0, local copies, waits for them, and re-layouts: 3.67 us -> none  [the longest x45 2.37 us: on_device(): moved = jnp.roll(moved, -vel[2], axis=2)]
  transfers between devices with their start and end apart: 13 -> 0, of which waited for: 10 -> 0; matrix products, arithmetic and copies ran while one was open for 4% -> 0% of each run, Pallas kernels for 0% -> 0%
where the time goes in v1:
time: 39.3 us; the launch traced here: 38.9 us
  Pallas kernels  30.7 us (78%)
  local copies, waits for them, and re-layouts  7.53 us (19%)
  between operations  0.65 us (2%)
    pallas_call x1, Pallas kernels, on_device(): pl.pallas_call(functools.partial(kernel, sizes), out_shape=(jax.ShapeDtyp...  30.7 us
    unnamed x13, local copies, waits for them, and re-layouts  7.53 us

profile of v1, /device:TPU:0, one launch (start us, length us, event | category | flops | bytes accessed | tf_op | source)
XLA Modules:
  0.0 38.9 jit_solution(13410655650748701942)
XLA Ops:
  0.6 0.9 %copy.8.span_ref = f32[256,32]{1,0:T(8,128)S(1)} copy(f32[256,32]{0,1:T(8,128)} %param.11) | data formatting | bytes 65536 | tf_op args[5]
  1.5 0.0 copy-start
  1.5 1.5 %copy-done = bf16[3,19,8,8,256]{4,3,2,1,0:T(8,128)(2,1)S(1)} copy-done((bf16[3,19,8,8,256]{4,3,2,1,0:T(8,128)(2,1)S(1)}, bf16[3,19,8,8,256]{4,3,2,1,0:T(8,128)(2,1)}, u32[]{:S(2)}) %copy-start) | copy-done | bytes 1867800
  3.0 0.0 copy-start.1
  3.0 1.3 %copy-done.1 = f32[19,8,8,256]{3,2,1,0:T(8,128)S(1)} copy-done((f32[19,8,8,256]{3,2,1,0:T(8,128)S(1)}, f32[19,8,8,256]{3,2,1,0:T(8,128)}, u32[]{:S(2)}) %copy-start.1) | copy-done | bytes 1245208
  4.3 0.0 copy-start.2
  4.3 0.8 %copy-done.2 = s32[8,8,256]{2,1,0:T(8,128)S(1)} copy-done((s32[8,8,256]{2,1,0:T(8,128)S(1)}, s32[8,8,256]{2,1,0:T(8,128)}, u32[]{:S(2)}) %copy-start.2) | copy-done | bytes 65560
  5.1 0.0 copy-start.3
  5.1 0.7 %copy-done.3 = f32[8,64]{1,0:T(8,128)S(1)} copy-done((f32[8,64]{1,0:T(8,128)S(1)}, f32[8,64]{1,0:T(8,128)}, u32[]{:S(2)}) %copy-start.3) | copy-done | bytes 2072
  5.8 0.0 copy-start.4
  5.8 0.7 %copy-done.4 = f32[8,64]{1,0:T(8,128)S(1)} copy-done((f32[8,64]{1,0:T(8,128)S(1)}, f32[8,64]{1,0:T(8,128)}, u32[]{:S(2)}) %copy-start.4) | copy-done | bytes 2072
  6.5 30.7 %shard_map.77 = (f32[19,8,8,256]{3,2,1,0:T(8,128)S(1)}, f32[4,32,32]{2,1,0:T(8,128)S(1)}) custom-call(bf16[3,19,8,8,256]{4,3,2,1,0:T(8,128)(2,1)S(1)} %copy-done, f32[19,8,8,256]{3,2,1,0:T(8,128)S(1)} %copy-done.1, s32[8,8,256]{2,1,0:T(8,128)S(1)} %copy-done.2, f32[8,64]{1,0:T(8,128)S(1)} %copy-done.3, f32[8,64]{1,0:T(8,128)S(1)} %copy-done.4, ...), custom_call_target="tpu_custom_call" | custom-call | flops 29491200 | bytes 5242880 | tf_op jit(solution)/shard_map/pallas_call | solution.py:457
  37.2 1.0 %copy.11 = f32[19,8,8,256]{3,2,1,0:T(8,128)} copy(f32[19,8,8,256]{3,2,1,0:T(8,128)S(1)} %get-tuple-element.4) | data formatting | bytes 2490368
  38.3 0.6 %copy.12 = f32[4,32,32]{2,1,0:T(8,128)} copy(f32[4,32,32]{2,1,0:T(8,128)S(1)} %get-tuple-element.5) | data formatting | bytes 32768
Async XLA Ops:
  1.5 1.5 %copy-start = (bf16[3,19,8,8,256]{4,3,2,1,0:T(8,128)(2,1)S(1)}, bf16[3,19,8,8,256]{4,3,2,1,0:T(8,128)(2,1)}, u32[]{:S(2)}) copy-start(bf16[3,19,8,8,256]{4,3,2,1,0:T(8,128)(2,1)} %fwd_hbm.1) | copy-start | bytes 5603332
  3.0 1.3 %copy-start.1 = (f32[19,8,8,256]{3,2,1,0:T(8,128)S(1)}, f32[19,8,8,256]{3,2,1,0:T(8,128)}, u32[]{:S(2)}) copy-start(f32[19,8,8,256]{3,2,1,0:T(8,128)} %adj_hbm.1) | copy-start | bytes 3735556
  4.3 0.8 %copy-start.2 = (s32[8,8,256]{2,1,0:T(8,128)S(1)}, s32[8,8,256]{2,1,0:T(8,128)}, u32[]{:S(2)}) copy-start(s32[8,8,256]{2,1,0:T(8,128)} %kind_ref.1) | copy-start | bytes 196612
  5.1 0.7 %copy-start.3 = (f32[8,64]{1,0:T(8,128)S(1)}, f32[8,64]{1,0:T(8,128)}, u32[]{:S(2)}) copy-start(f32[8,64]{1,0:T(8,128)} %len_ref.1) | copy-start | bytes 6148
  5.8 0.7 %copy-start.4 = (f32[8,64]{1,0:T(8,128)S(1)}, f32[8,64]{1,0:T(8,128)}, u32[]{:S(2)}) copy-start(f32[8,64]{1,0:T(8,128)} %dep_ref.1) | copy-start | bytes 6148

commit v2 on v1

--- a/solution.py
+++ b/solution.py
@@ -55,6 +55,14 @@
     )
 
 
+def quotient(a, n):
+    return a >> (n.bit_length() - 1) if n & (n - 1) == 0 else lax.div(a, n)
+
+
+def remainder(a, n):
+    return a & (n - 1) if n & (n - 1) == 0 else lax.rem(a, n)
+
+
 def one_hot(shape, test):
     rows = lax.broadcasted_iota(jnp.int32, shape, 0)
     cols = lax.broadcasted_iota(jnp.int32, shape, 1)
@@ -65,11 +73,11 @@
     sizes,
     fwd_hbm,
     adj_hbm,
-    kind_ref,
-    len_ref,
-    dep_ref,
-    span_ref,
-    out_ref,
+    kind_hbm,
+    len_hbm,
+    dep_hbm,
+    span_hbm,
+    out_hbm,
     coef_ref,
     adj,
     fwd,
@@ -86,8 +94,15 @@
     depgot,
     span_wide,
     len_wide,
+    kind_ref,
+    len_ref,
+    dep_ref,
+    span_ref,
+    out_ref,
     load_sem,
     fwd_sem,
+    small_sem,
+    out_sem,
     x_sems,
     y_sems,
     c_sems,
@@ -114,6 +129,14 @@
         for k, i in enumerate(ORDER)
     ]
     for copy in loads:
+        copy.start()
+    small = [
+        pltpu.make_async_copy(src, dst, small_sem.at[k])
+        for k, (src, dst) in enumerate(
+            ((dep_hbm, dep_ref), (kind_hbm, kind_ref), (len_hbm, len_ref), (span_hbm, span_ref))
+        )
+    ]
+    for copy in small:
         copy.start()
     fwd_loads = [
         pltpu.make_async_copy(fwd_hbm.at[t], fwd.at[t], fwd_sem.at[t]) for t in range(STEPS)
@@ -205,6 +228,8 @@
     fill_corners(0)
     pl.semaphore_wait(barrier, len(peers))
     send(0)
+    for copy in small:
+        copy.wait()
     basis_copies = [
         remote(dep_ref, depgot.at[k], b_sems, (k,), device(0, k)) for k in range(1, count_dep)
     ]
@@ -335,19 +360,19 @@
             store(o, jnp.where(solid, post[i], (1.0 - omega) * post[o] + (acc_rho - grad)))
 
     prepare(STEPS - 1)
-    spread = one_hot((mz, 128), lambda r, c: lax.rem(c, mz) == r)
-    span_wide[...] = exact_dot(span_ref[...], spread)
+    spread = one_hot((mz, 128), lambda r, c: remainder(c, mz) == r)
+    span_wide[...] = exact_dot(span_ref[...], spread, ((0,), (0,)))
     total = count_len * piece
     pick = one_hot(
         (total, mx),
-        lambda r, c: (lax.div(r, piece) * own_p + lax.div(lax.rem(r, piece), highs) == c)
-        & (lax.rem(r, piece) < own_p * highs),
+        lambda r, c: (quotient(r, piece) * own_p + quotient(remainder(r, piece), highs) == c)
+        & (remainder(r, piece) < own_p * highs),
     )
     lens = exact_dot(pick, len_ref[...], ((1,), (1,)))
-    cells = one_hot((nx, nx * ny), lambda r, c: lax.div(c, ny) == r)
+    cells = one_hot((nx, nx * ny), lambda r, c: quotient(c, ny) == r)
     halves = one_hot(
         (total, nx * ny),
-        lambda r, c: lax.div(lax.rem(c, ny), fold) == lax.rem(lax.rem(r, piece), highs),
+        lambda r, c: quotient(remainder(c, ny), fold) == remainder(remainder(r, piece), highs),
     )
     len_wide[...] = exact_dot(lens, cells) * halves
 
@@ -376,7 +401,7 @@
 
     narrow = exact_dot(sens[...], span_wide[...])
     keep = one_hot(
-        (nx * ny, 128), lambda r, c: lax.rem(lax.rem(r, ny), fold) == lax.div(c, mz)
+        (nx * ny, 128), lambda r, c: remainder(remainder(r, ny), fold) == quotient(c, mz)
     )
     partial = exact_dot(len_wide[...], narrow * keep)
     tbuf[...] = partial.reshape(tbuf.shape)
@@ -386,20 +411,22 @@
     ]
     for copy in t_copies:
         copy.start()
+    out_copy = pltpu.make_async_copy(out_ref, out_hbm, out_sem)
+    out_copy.start()
 
     for copy in basis_copies:
         copy.wait_recv()
     width = fold * piece
     mine = one_hot(
-        (own_p * own_q, my), lambda r, c: lax.rem(r, own_q) + at_dep * own_q == c
+        (own_p * own_q, my), lambda r, c: remainder(r, own_q) + at_dep * own_q == c
     )
     lay = one_hot(
         (ny, width),
-        lambda r, c: lax.rem(lax.rem(c, piece), highs) * fold + lax.div(c, piece) == r,
+        lambda r, c: remainder(remainder(c, piece), highs) * fold + quotient(c, piece) == r,
     )
     match = one_hot(
         (own_p * own_q, width),
-        lambda r, c: lax.div(lax.rem(c, piece), highs) == lax.div(r, own_q),
+        lambda r, c: quotient(remainder(c, piece), highs) == quotient(r, own_q),
     )
     deps = [
         exact_dot(
@@ -439,6 +466,7 @@
                 copy.wait_send()
     for copy in basis_copies + t_copies + r_copies:
         copy.wait_send()
+    out_copy.wait()
 
 
 def on_device(forward_states, adjoint_end, cell_kind, basis_len, basis_dep, basis_span):
@@ -460,8 +488,8 @@
             jax.ShapeDtypeStruct((COUNT, nx, ny, nz), f32),
             jax.ShapeDtypeStruct((own_p, my // count_dep, mz), f32),
         ),
-        in_specs=[hbm, hbm, vmem, vmem, vmem, vmem],
-        out_specs=(vmem, vmem),
+        in_specs=[hbm] * 6,
+        out_specs=(hbm, vmem),
         scratch_shapes=[
             pltpu.VMEM((STEPS, COUNT, nx + 2, ny, nz), f32),
             pltpu.VMEM(forward_states.shape, forward_states.dtype),
@@ -478,8 +506,15 @@
             pltpu.VMEM((count_dep, ny, my), f32),
             pltpu.VMEM((nz, 128), f32),
             pltpu.VMEM((count_len * piece, nx * ny), f32),
+            pltpu.VMEM(cell_kind.shape, cell_kind.dtype),
+            pltpu.VMEM(basis_len.shape, f32),
+            pltpu.VMEM(basis_dep.shape, f32),
+            pltpu.VMEM((mz, nz), f32),
+            pltpu.VMEM((COUNT, nx, ny, nz), f32),
             dma,
             dma((STEPS,)),
+            dma((4,)),
+            dma,
             dma((2, STEPS, 2)),
             dma((2, STEPS, 2)),
             dma((2, STEPS, 4)),
@@ -488,12 +523,12 @@
             dma((2, count_dep)),
         ],
         compiler_params=pltpu.CompilerParams(
-            collective_id=0, has_side_effects=True, vmem_limit_bytes=48 * 1024 * 1024
+            collective_id=0, has_side_effects=True, vmem_limit_bytes=62 * 1024 * 1024
         ),
         cost_estimate=pl.CostEstimate(
             flops=STEPS * 600 * nx * ny * nz, bytes_accessed=5 * 1024 * 1024, transcendentals=0
         ),
-    )(forward_states, adjoint_end, cell_kind, basis_len, basis_dep, basis_span)
+    )(forward_states, adjoint_end, cell_kind, basis_len, basis_dep, basis_span.T)
 
 
 def solution(mesh):

time: 39.3 us -> 33.3 us (0.85)
  local copies, waits for them, and re-layouts: 7.53 us -> 3.11 us
  Pallas kernels: 30.7 us -> 29.4 us
    unnamed x13 -> x4, local copies, waits for them, and re-layouts: 7.53 us -> 3.11 us
    pallas_call x1, Pallas kernels: 30.7 us -> 29.4 us  [on_device(): pl.pallas_call(functools.partial(kernel, sizes), out_shape=(jax.ShapeDtyp...]
where the time goes in v2:
time: 33.3 us; the launch traced here: 33.1 us
  Pallas kernels  29.4 us (88%)
  local copies, waits for them, and re-layouts  3.11 us (9%)
  between operations  0.65 us (2%)
    pallas_call x1, Pallas kernels, on_device(): pl.pallas_call(functools.partial(kernel, sizes), out_shape=(jax.ShapeDtyp...  29.4 us
    unnamed x4, local copies, waits for them, and re-layouts  3.11 us

profile of v2, /device:TPU:0, one launch (start us, length us, event | category | flops | bytes accessed | tf_op | source)
XLA Modules:
  0.0 33.1 jit_solution(9810165195514645123)
XLA Ops:
  0.6 29.4 %shard_map.77 = (f32[19,8,8,256]{3,2,1,0:T(8,128)}, f32[4,32,32]{2,1,0:T(8,128)}) custom-call(bf16[3,19,8,8,256]{4,3,2,1,0:T(8,128)(2,1)} %fwd_hbm.1, f32[19,8,8,256]{3,2,1,0:T(8,128)} %adj_hbm.1, s32[8,8,256]{2,1,0:T(8,128)} %kind_hbm.1, f32[8,64]{1,0:T(8,128)} %len_hbm.1, f32[8,64]{1,0:T(8,128)} %dep_hbm.1, f32[32,256]{1,0:T(8,128)} %bitcast.1), custom_call_target="tpu_custom_call" | custom-call | flops 29491200 | bytes 5242880 | tf_op jit(solution)/shard_map/pallas_call | solution.py:485
  30.0 0.0 copy-start
  30.0 2.5 %copy.10 = f32[19,8,8,256]{3,2,1,0:T(8,128)} copy(f32[19,8,8,256]{3,2,1,0:T(8,128)} %get-tuple-element.4) | data formatting | bytes 2490368
  32.5 0.0 copy-done
  32.5 0.6 %copy.11 = f32[4,32,32]{2,1,0:T(8,128)} copy(f32[4,32,32]{2,1,0:T(8,128)S(1)} %copy-done) | data formatting | bytes 32768
Async XLA Ops:
  30.0 2.5 %copy-start = (f32[4,32,32]{2,1,0:T(8,128)S(1)}, f32[4,32,32]{2,1,0:T(8,128)}, u32[]{:S(2)}) copy-start(f32[4,32,32]{2,1,0:T(8,128)} %get-tuple-element.5) | copy-start | bytes 49156

commit v3 on v2

--- a/solution.py
+++ b/solution.py
@@ -469,6 +469,24 @@
     out_copy.wait()
 
 
+def hand_over(adj_in, coef_in, adj_out, coef_out, adj_held, coef_held, sems):
+    parts = [(coef_in, coef_held, coef_out)]
+    parts += [(adj_in.at[i], adj_held.at[i], adj_out.at[i]) for i in range(COUNT)]
+    reads = [
+        pltpu.make_async_copy(src, mid, sems.at[0, k]) for k, (src, mid, dst) in enumerate(parts)
+    ]
+    writes = [
+        pltpu.make_async_copy(mid, dst, sems.at[1, k]) for k, (src, mid, dst) in enumerate(parts)
+    ]
+    for read in reads:
+        read.start()
+    for read, write in zip(reads, writes):
+        read.wait()
+        write.start()
+    for write in writes:
+        write.wait()
+
+
 def on_device(forward_states, adjoint_end, cell_kind, basis_len, basis_dep, basis_span):
     count_len = lax.axis_size("len")
     count_dep = lax.axis_size("dep")
@@ -482,7 +500,7 @@
     dma = pltpu.SemaphoreType.DMA
     vmem = pl.BlockSpec(memory_space=pltpu.VMEM)
     hbm = pl.BlockSpec(memory_space=pl.ANY)
-    return pl.pallas_call(
+    adjoint, coefficients = pl.pallas_call(
         functools.partial(kernel, sizes),
         out_shape=(
             jax.ShapeDtypeStruct((COUNT, nx, ny, nz), f32),
@@ -529,6 +547,21 @@
             flops=STEPS * 600 * nx * ny * nz, bytes_accessed=5 * 1024 * 1024, transcendentals=0
         ),
     )(forward_states, adjoint_end, cell_kind, basis_len, basis_dep, basis_span.T)
+    return pl.pallas_call(
+        hand_over,
+        out_shape=(
+            jax.ShapeDtypeStruct(adjoint.shape, f32),
+            jax.ShapeDtypeStruct(coefficients.shape, f32),
+        ),
+        in_specs=[hbm, hbm],
+        out_specs=(hbm, hbm),
+        scratch_shapes=[
+            pltpu.VMEM(adjoint.shape, f32),
+            pltpu.VMEM(coefficients.shape, f32),
+            dma((2, COUNT + 1)),
+        ],
+        compiler_params=pltpu.CompilerParams(vmem_limit_bytes=62 * 1024 * 1024),
+    )(adjoint, coefficients)
 
 
 def solution(mesh):

time: 33.3 us -> 32.5 us (0.976)
  local copies, waits for them, and re-layouts: 3.11 us -> 0 us
  Pallas kernels: 29.4 us -> 31.7 us
    unnamed x4 -> x0, local copies, waits for them, and re-layouts: 3.11 us -> none
    pallas_call x0 -> x1, Pallas kernels: none -> 2.31 us  [on_device(): pl.pallas_call(hand_over, out_shape=(jax.ShapeDtypeStruct(adjoint.shape,...]
where the time goes in v3:
time: 32.5 us; the launch traced here: 32.3 us
  Pallas kernels  31.7 us (98%)
  between operations  0.64 us (2%)
    pallas_call x1, Pallas kernels, on_device(): pl.pallas_call(functools.partial(kernel, sizes), out_shape=(jax.ShapeDtyp...  29.4 us
    pallas_call x1, Pallas kernels, on_device(): pl.pallas_call(hand_over, out_shape=(jax.ShapeDtypeStruct(adjoint.shape,...  2.31 us

profile of v3, /device:TPU:0, one launch (start us, length us, event | category | flops | bytes accessed | tf_op | source)
XLA Modules:
  0.0 32.3 jit_solution(17515608285373074477)
XLA Ops:
  0.6 29.4 %shard_map.77 = (f32[19,8,8,256]{3,2,1,0:T(8,128)}, f32[4,32,32]{2,1,0:T(8,128)}) custom-call(bf16[3,19,8,8,256]{4,3,2,1,0:T(8,128)(2,1)} %fwd_hbm.1, f32[19,8,8,256]{3,2,1,0:T(8,128)} %adj_hbm.1, s32[8,8,256]{2,1,0:T(8,128)} %kind_hbm.1, f32[8,64]{1,0:T(8,128)} %len_hbm.1, f32[8,64]{1,0:T(8,128)} %dep_hbm.1, f32[32,256]{1,0:T(8,128)} %bitcast.1), custom_call_target="tpu_custom_call" | custom-call | flops 29491200 | bytes 5242880 | tf_op jit(solution)/shard_map/pallas_call | solution.py:503
  30.0 2.3 %shard_map.78 = (f32[19,8,8,256]{3,2,1,0:T(8,128)}, f32[4,32,32]{2,1,0:T(8,128)}) custom-call(f32[19,8,8,256]{3,2,1,0:T(8,128)} %get-tuple-element.4.adj_in, f32[4,32,32]{2,1,0:T(8,128)} %get-tuple-element.5.coef_in), custom_call_target="tpu_custom_call" | custom-call | tf_op jit(solution)/shard_map/pallas_call | solution.py:550
